TPU v7x, 512 devices: a whole 4x4x16 slice. The times are simulated.
512 devices in a mesh: det: 64 (over x, z), tm: 8 (over y, core).
Axes of the slice: x: 4, y: 4, z: 16, core: 2. Of those that a mesh axis runs over, the one named last changes fastest.
Arguments:
- timestream: bfloat16 [8192, 1024], P('det', 'tm'), may hold values from -6 to 6
- pointing: int32 [8192, 1024], P('det', 'tm'), may hold values from 0 to 65535
- detector_band: int32 [8192], P('det'), may hold values from 0 to 19
- mode_loading: bfloat16 [8192, 64], P('det'), may hold values from -0.29492188 to 0.29492188
- mode_mix: float32 [20, 64, 64], replicated, may hold values from -0.36 to 0.36
- noise_weight: float32 [8192], P('det'), may hold values from 0.3 to 3
- ownership: int32 [512], replicated, may hold values from 0 to 511, each once
Outputs:
- amplitudes: float32 [1280, 1024], P(None, 'tm')
- sky_map: float32 [512, 128], P('det')
Inputs may be any that keep to these rules, and one draw needn't show every extreme that they name: `ownership`: each tile appears once.
All inputs are finite; a program needn't handle non-finite values.
Results may differ from a plain program's by a relative error of at most 0.0037.
Values sent between devices are 32-bit elements; how exact they have to be, the bound alone decides.
No kernel may reach another device: no remote copies, remote signals or barrier semaphores. Data moves between devices by JAX's collectives and lax.ppermute only.
A program may use at most 64 MiB of HBM per device.

v0:
```python
import functools

import jax
import jax.numpy as jnp
from jax import lax
from jax.experimental import pallas as pl
from jax.experimental.pallas import tpu as pltpu
from jax.sharding import Mesh, PartitionSpec as P

TILE_PIX = 128
HALF = 256
GROUP = 8
EXTRA = 8
F32 = jnp.float32
BF16 = jnp.bfloat16


def lanes(rows, width):
    return lax.broadcasted_iota(jnp.int32, (rows, 128), 1) // width


def turn(x, amount):
    amount %= 128
    return pltpu.roll(x, amount, 1) if amount else x


def split(x):
    high = x.astype(BF16)
    low = (x - high.astype(F32)).astype(BF16)
    return high, low


def pack_kernel(nx, *refs):
    sources, (out_ref, *held, sems) = refs[:5], refs[5:]
    copies = [
        pltpu.make_async_copy(src, dst, sems.at[n]) for n, (src, dst) in enumerate(zip(sources, held))
    ]
    for copy in copies:
        copy.start()
    for copy in copies:
        copy.wait()
    loading_t_ref, band_ref, noise_ref, ts_ref, point_ref = held
    modes, dets = loading_t_ref.shape
    width = ts_ref.shape[1] // nx
    rows = dets + EXTRA
    ts = ts_ref[...].astype(F32)
    point = point_ref[...].astype(F32)
    loading_t = loading_t_ref[...].astype(F32)
    loading = jnp.concatenate([jnp.zeros((128 - modes, dets), F32), loading_t], axis=0).T
    group = lanes(dets, width)
    for d in range(nx):
        body = jnp.where(group == 0, turn(ts, -width * d), turn(point, width - width * d))
        out_ref[d * rows:d * rows + dets, :] = jnp.where(group < 2, body, loading)
        out_ref[d * rows + dets:(d + 1) * rows, :] = jnp.concatenate(
            [band_ref[...].astype(F32), noise_ref[...], jnp.zeros((EXTRA - 2, dets), F32)], axis=0
        )


def project_kernel(nx, modes, pad, got_ref, out_ref):
    rows = got_ref.shape[0] // nx
    dets = rows - EXTRA
    width = 128 // nx
    per = modes * width // 128
    group = lanes(dets, width)
    slot = lax.broadcasted_iota(jnp.int32, (pad, dets), 0).astype(F32)
    left, right = [], []
    for s in range(nx):
        chunk = got_ref[s * rows:s * rows + dets, :]
        loading_t = chunk.T[128 - modes:, :]
        ts = jnp.where(group == 0, chunk, 0.0)
        pick = jnp.where(slot == got_ref[s * rows + dets:s * rows + dets + 1, :], 1.0, 0.0)
        for j in range(modes // per):
            part = loading_t[j * per:(j + 1) * per, :]
            left.append((part[:, None, :] * pick[None]).reshape(per * pad, dets).astype(BF16))
            right.append(turn(ts, width * j).astype(BF16))
    out_ref[...] = jnp.dot(
        jnp.concatenate(left, axis=1), jnp.concatenate(right, axis=0), preferred_element_type=F32
    )


def row(ref, i, times):
    return jnp.broadcast_to(ref[pl.ds(i, 1), :], (16, times)).astype(BF16)[None]


def add_bins(value_ref, hi_ref, lo_ref, acc_ref):
    dets, times = value_ref.shape
    ids = lax.broadcasted_iota(jnp.int32, (HALF, times), 0).astype(F32).astype(BF16)
    ids = ids.reshape(HALF // 16, 16, times)
    one = jnp.ones((), BF16)
    zero = jnp.zeros((), BF16)

    def body(g, carry):
        left, right = [], []
        for k in range(GROUP):
            i = g * GROUP + k
            upper = row(hi_ref, i, times) == ids
            lower = row(lo_ref, i, times) == ids
            left.append(jnp.where(upper, one, zero).reshape(HALF, times))
            right.append(jnp.where(lower, row(value_ref, i, times), zero).reshape(HALF, times))
        added = lax.dot_general(
            jnp.concatenate(left, axis=1),
            jnp.concatenate(right, axis=1),
            (((1,), (1,)), ((), ())),
            preferred_element_type=F32,
        )
        acc_ref[:HALF, :] += added[:, :TILE_PIX]
        acc_ref[HALF:, :] += added[:, TILE_PIX:]
        return carry

    lax.fori_loop(0, dets // GROUP, body, 0, unroll=4)


def weighted_kernel(
    nx, bands, modes, got_ref, wide_ref, noise_ref, hi_ref, lo_ref, acc_ref, value_s
):
    rows = got_ref.shape[0] // nx
    dets = rows - EXTRA
    width = 128 // nx
    group = lanes(dets, width)
    half = lanes(dets, modes)
    for s in range(nx):
        chunk = got_ref[s * rows:s * rows + dets, :]
        tail = got_ref[s * rows + dets:(s + 1) * rows, :]
        columns = jnp.concatenate([tail, jnp.zeros((128 - EXTRA, dets), F32)], axis=0).T
        band_off = jnp.broadcast_to(columns[:, 0:1], (dets, 128)) - half.astype(F32)
        loading2 = jnp.where(half == 0, turn(chunk, modes), chunk)
        for b in range(0, bands, 2):
            wide_ref[s * dets:(s + 1) * dets, b * modes:(b + 2) * modes] = jnp.where(
                band_off == float(b), loading2, 0.0
            ).astype(BF16)
        here = (
            jnp.broadcast_to(columns[:, 1:2], (dets, 128)),
            turn(chunk, width * s),
            turn(chunk, width * (s - 1)),
        )
        total = here if s == 0 else tuple(
            jnp.where(group == s, a, b) for a, b in zip(here, total)
        )
    noise, ts, point = total
    noise_ref[...] = noise
    value_s[...] = (noise * ts).astype(BF16).astype(F32)
    point = point.astype(jnp.int32)
    hi_ref[...] = (point >> 8).astype(F32)
    lo_ref[...] = (point & 255).astype(F32)
    acc_ref[...] = jnp.zeros_like(acc_ref)
    add_bins(value_s, hi_ref, lo_ref, acc_ref)


def correct_kernel(
    nx, bands, pad, own_ref, proj_ref, mix_ref, wide_ref, noise_ref, hi_ref, lo_ref, start_ref,
    amp_ref, map_ref, value_s, acc_s
):
    modes = mix_ref.shape[1]
    dets = noise_ref.shape[0]
    width = 128 // nx
    per = modes // nx
    group = lanes(per, width)
    rounded = []
    for b in range(bands):
        mine = proj_ref[pl.ds(b, per, stride=pad), :]
        turned = [turn(mine, width * k) for k in range(nx)]
        pieces = []
        for j in range(nx):
            piece = turned[(0 - j) % nx]
            for g in range(1, nx):
                piece = jnp.where(group == g, turned[(g - j) % nx], piece)
            pieces.append(piece)
        p = jnp.concatenate(pieces, axis=0)
        mh, ml = split(mix_ref[b])
        ph, plow = split(p)
        amp = p + jnp.dot(
            jnp.concatenate([mh, ml, mh], axis=1),
            jnp.concatenate([ph, ph, plow], axis=0),
            preferred_element_type=F32,
        )
        rounded.append(amp.astype(BF16))
        packed = amp[:per, :]
        for j in range(1, nx):
            packed = jnp.where(group == j, amp[j * per:(j + 1) * per, :], packed)
        amp_ref[b * per:(b + 1) * per, :] = packed
    fits = jnp.dot(wide_ref[...], jnp.concatenate(rounded, axis=0), preferred_element_type=F32)
    group = lanes(dets, width)
    fitted = fits[:dets, :]
    for s in range(1, nx):
        fitted = jnp.where(group == s, fits[s * dets:(s + 1) * dets, :], fitted)
    value_s[...] = -(noise_ref[...] * fitted).astype(BF16).astype(F32)
    acc_s[...] = start_ref[...]
    add_bins(value_s, hi_ref, lo_ref, acc_s)
    for r in range(map_ref.shape[0]):
        tile = own_ref[r]
        map_ref[r:r + 1, :] = acc_s[pl.ds((tile & 1) * HALF + (tile >> 1), 1), :]


def gather_kernel(nx, bands, *refs):
    parts, out_ref = refs[:nx], refs[nx]
    per = parts[0].shape[0] // bands
    width = 128 // nx
    group = lanes(per, width)
    mine = lax.axis_index("x")
    sources = [lax.rem(mine + nx - k, nx) for k in range(nx)]
    for b in range(bands):
        for j in range(nx):
            total = jnp.zeros((per, 128), F32)
            for k in range(nx):
                piece = parts[k][b * per:(b + 1) * per, :]
                moved = pltpu.roll(piece, lax.rem(sources[k] + nx - j, nx) * width, 1)
                total = jnp.where(group == sources[k], moved, total)
            out_ref[(b * nx + j) * per:(b * nx + j + 1) * per, :] = total


def add_over(x, axes):
    swapped = lax.all_to_all(x, axes, 0, 0, tiled=True)
    return swapped.reshape((lax.axis_size(axes), -1) + x.shape[1:]).sum(0)


def copy_over(x, axes):
    count = lax.axis_size(axes)
    spread = jnp.broadcast_to(x[None], (count,) + x.shape).reshape((-1,) + x.shape[1:])
    return lax.all_to_all(spread, axes, 0, 0, tiled=True)


def per_device(
    timestream, pointing, detector_band, mode_loading, mode_mix, noise_weight, ownership
):
    dets, times = timestream.shape
    bands, modes = mode_mix.shape[:2]
    pad = -(-bands // 8) * 8
    tiles = ownership.shape[0]
    nx, nh, nl = lax.axis_size("x"), lax.axis_size("zh"), lax.axis_size("zl")
    nz = nh * nl
    nt = lax.axis_size("y") * lax.axis_size("core")
    vmem = pl.BlockSpec(memory_space=pltpu.VMEM)
    smem = pl.BlockSpec(memory_space=pltpu.SMEM)
    params = pltpu.CompilerParams(vmem_limit_bytes=32 * 1024 * 1024)

    bin_cost = pl.CostEstimate(
        flops=2 * dets * times * HALF * HALF, bytes_accessed=1 << 21, transcendentals=0
    )

    def call(kernel, shapes, args, specs=None, scratch=(), cost=None, limit=params, types=None):
        return pl.pallas_call(
            kernel,
            out_shape=tuple(
                jax.ShapeDtypeStruct(s, t) for s, t in zip(shapes, types or [F32] * len(shapes))
            ),
            in_specs=specs or [vmem] * len(args),
            out_specs=tuple(vmem for _ in shapes),
            scratch_shapes=scratch,
            compiler_params=limit,
            cost_estimate=cost,
        )(*args)

    inputs = (mode_loading.T, detector_band[None, :], noise_weight[None, :], timestream, pointing)
    (packed,) = call(
        functools.partial(pack_kernel, nx),
        [(nx * (dets + EXTRA), 128)],
        inputs,
        specs=[pl.BlockSpec(memory_space=pltpu.HBM)] * 5,
        scratch=[pltpu.VMEM(a.shape, a.dtype) for a in inputs] + [pltpu.SemaphoreType.DMA((5,))],
        limit=None,
    )
    got = lax.all_to_all(packed, "x", 0, 0, tiled=True)
    (local,) = call(
        functools.partial(project_kernel, nx, modes, pad), [(nz * pad, 128)], (got,)
    )
    share, got = lax.optimization_barrier((add_over(local, "zl"), got))
    wide, noise, hi, lo, start = call(
        functools.partial(weighted_kernel, nx, bands, modes),
        [(nx * dets, bands * modes)] + [(dets, times)] * 3 + [(2 * HALF, TILE_PIX)],
        (got,),
        scratch=[pltpu.VMEM((dets, times), F32)],
        cost=bin_cost,
        types=[BF16] + [F32] * 4,
    )
    share = copy_over(share, "zh").reshape((nh,) + share.shape).sum(0)
    share, wide, noise, hi, lo, start = lax.optimization_barrier((share, wide, noise, hi, lo, start))
    projected = copy_over(share, "zl")
    amp, part = call(
        functools.partial(correct_kernel, nx, bands, pad),
        [(bands * modes // nx, 128), (tiles, TILE_PIX)],
        (ownership, projected, mode_mix, wide, noise, hi, lo, start),
        specs=[smem] + [vmem] * 7,
        scratch=[pltpu.VMEM((dets, times), F32), pltpu.VMEM((2 * HALF, TILE_PIX), F32)],
        cost=bin_cost,
    )
    moved = [
        lax.ppermute(amp, "x", [(i, (i + k) % nx) for i in range(nx)]) for k in range(1, nx)
    ]
    (amplitudes,) = call(
        functools.partial(gather_kernel, nx, bands), [(bands * modes, times)], (amp, *moved)
    )
    share = add_over(part, ("x", "zh", "zl"))
    share, amplitudes = lax.optimization_barrier((share, amplitudes))
    sky_map = copy_over(share, ("y", "core")).reshape((nt,) + share.shape).sum(0)
    return amplitudes, sky_map


def solution(mesh):
    fine = Mesh(mesh.devices.reshape(4, 4, 4, 4, 2), ("x", "zh", "zl", "y", "core"))
    det, tm = ("x", "zh", "zl"), ("y", "core")
    placed = (P(det, tm), P(det, tm), P(det), P(det, None), P(), P(det), P())
    return jax.shard_map(
        per_device,
        mesh=fine,
        in_specs=placed,
        out_specs=(P(None, tm), P(det, None)),
        check_vma=False,
    )
```

profile of v0, /device:TPU:1, one launch (start us, length us, event | category | flops | bytes accessed | tf_op | source)
XLA Modules:
  0.0 105.1 jit_solution(14179685719479737008)
XLA Ops:
  0.6 1.8 %shard_map.86 = f32[544,128]{1,0:T(8,128)} custom-call(bf16[64,128]{1,0:T(8,128)(2,1)} %bitcast.13, s32[1,128]{1,0:T(1,128)} %bitcast.14, f32[1,128]{1,0:T(1,128)} %bitcast.15, bf16[128,128]{1,0:T(8,128)(2,1)} %refs_3_.1, s32[128,128]{1,0:T(8,128)} %refs_4_.1), custom_call_target="tpu_custom_call" | custom-call | tf_op jit(solution)/shard_map/pallas_call | solution.py:241
  2.5 10.5 %all_to_all.49 = f32[4,136,128]{2,1,0:T(8,128)S(1)} all-to-all(f32[4,136,128]{2,1,0:T(8,128)} %bitcast.12), channel_id=1, replica_groups=mesh['x'=4,'zh'=4,'zl'=4,'y'=4,'core'=2] {'x'}, dimensions={0} | all-to-all | bytes 557056 | tf_op jit(solution)/shard_map/all_to_all | solution.py:262
  12.9 0.7 shard_map.87
  13.6 11.1 %all_to_all.50 = f32[4,96,128]{2,1,0:T(8,128)S(1)} all-to-all(f32[4,96,128]{2,1,0:T(8,128)S(1)} %bitcast.10), channel_id=1, replica_groups=mesh['x'=4,'zh'=4,'zl'=4,'y'=4,'core'=2] {'zl'}, dimensions={0} | all-to-all | bytes 393216 | tf_op jit(solution)/shard_map/all_to_all | solution.py:212
  24.7 0.7 broadcast_in_dim.12
  25.4 12.1 %all-to-all-start.2 = ((f32[4,96,128]{2,1,0:T(8,128)}), f32[4,96,128]{2,1,0:T(8,128)S(1)}, u32[]{:S(2)}, u32[]{:S(2)}) async-start(f32[4,96,128]{2,1,0:T(8,128)} %broadcast_in_dim.12), calls=%async_computation.2 | async-start | bytes 393216 | tf_op jit(solution)/shard_map/all_to_all | solution.py:219
  37.5 0.0 copy-start
  37.5 0.0 copy-start.1
  37.5 3.6 %shard_map.88 = (bf16[512,1280]{1,0:T(8,128)(2,1)S(1)}, f32[128,128]{1,0:T(8,128)S(1)}, f32[128,128]{1,0:T(8,128)S(1)}, f32[128,128]{1,0:T(8,128)S(1)}, f32[512,128]{1,0:T(8,128)S(1)}) custom-call(f32[544,128]{1,0:T(8,128)S(1)} %bitcast.9), custom_call_target="tpu_custom_call" | custom-call | flops 2147483648 | bytes 2097152 | tf_op jit(solution)/shard_map/pallas_call | solution.py:241
  41.2 9.1 %all-to-all-done.2 = f32[4,96,128]{2,1,0:T(8,128)S(1)} async-done(((f32[4,96,128]{2,1,0:T(8,128)}), f32[4,96,128]{2,1,0:T(8,128)S(1)}, u32[]{:S(2)}, u32[]{:S(2)}) %all-to-all-start.2) | async-done | bytes 196640 | tf_op jit(solution)/shard_map/all_to_all | solution.py:219
  50.3 8.6 %all_to_all.51 = f32[4,96,128]{2,1,0:T(8,128)S(1)} all-to-all(f32[4,96,128]{2,1,0:T(8,128)S(1)} %broadcast_in_dim.13), channel_id=1, replica_groups=mesh['x'=4,'zh'=4,'zl'=4,'y'=4,'core'=2] {'zl'}, dimensions={0} | all-to-all | bytes 393216 | tf_op jit(solution)/shard_map/all_to_all | solution.py:219
  58.9 0.0 copy-done
  58.9 0.0 copy-done.1
  58.9 6.0 %shard_map.89 = (f32[320,128]{1,0:T(8,128)S(1)}, f32[512,128]{1,0:T(8,128)}) custom-call(s32[512]{0:T(512)S(1)} %copy-done.1, f32[384,128]{1,0:T(8,128)S(1)} %bitcast.11, f32[20,64,64]{2,1,0:T(8,128)S(1)} %copy-done, bf16[512,1280]{1,0:T(8,128)(2,1)S(1)} %get-tuple-element.27.wide_ref, f32[128,128]{1,0:T(8,128)S(1)} %get-tuple-element.28.noise_ref, ...), custom_call_target="tpu_custom_call" | custom-call | flops 2147483648 | bytes 2097152 | tf_op jit(solution)/shard_map/pallas_call | solution.py:241
  65.0 5.9 %all-to-all-start.4 = ((f32[64,8,128]{2,1,0:T(8,128)}), f32[64,8,128]{2,1,0:T(8,128)S(1)}, u32[]{:S(2)}, u32[]{:S(2)}) async-start(f32[64,8,128]{2,1,0:T(8,128)} %bitcast.7), calls=%async_computation.4 | async-start | bytes 524288 | tf_op jit(solution)/shard_map/all_to_all | solution.py:212
  70.8 4.3 %collective-permute-start.2 = (f32[320,128]{1,0:T(8,128)S(1)}, f32[320,128]{1,0:T(8,128)S(1)}, u32[]{:S(2)}, u32[]{:S(2)}) collective-permute-start(f32[320,128]{1,0:T(8,128)S(1)} %get-tuple-element.33.refs_0_), channel_id=1, source_target_pairs={{0,384},{128,0},{256,128},{384,256},{1,385},{129,1},{257,129},{385... | collective-permute-start | bytes 491528 | tf_op jit(solution)/shard_map/ppermute | solution.py:287
  75.2 2.3 %collective-permute-start.1 = (f32[320,128]{1,0:T(8,128)S(1)}, f32[320,128]{1,0:T(8,128)S(1)}, u32[]{:S(2)}, u32[]{:S(2)}) collective-permute-start(f32[320,128]{1,0:T(8,128)S(1)} %get-tuple-element.33.refs_0_), channel_id=1, source_target_pairs={{0,256},{128,384},{256,0},{384,128},{1,257},{129,385},{257,1},{385... | collective-permute-start | bytes 491528 | tf_op jit(solution)/shard_map/ppermute | solution.py:287
  77.5 2.6 %collective-permute-start = (f32[320,128]{1,0:T(8,128)S(1)}, f32[320,128]{1,0:T(8,128)S(1)}, u32[]{:S(2)}, u32[]{:S(2)}) collective-permute-start(f32[320,128]{1,0:T(8,128)S(1)} %get-tuple-element.33.refs_0_), channel_id=1, source_target_pairs={{0,128},{128,256},{256,384},{384,0},{1,129},{129,257},{257,385},{3... | collective-permute-start | bytes 491528 | tf_op jit(solution)/shard_map/ppermute | solution.py:287
  80.0 0.0 collective-permute-done.2.refs_3_
  80.1 3.3 %collective-permute-done.1.refs_2_ = f32[320,128]{1,0:T(8,128)S(1)} collective-permute-done((f32[320,128]{1,0:T(8,128)S(1)}, f32[320,128]{1,0:T(8,128)S(1)}, u32[]{:S(2)}, u32[]{:S(2)}) %collective-permute-start.1) | collective-permute-done | bytes 163872 | tf_op jit(solution)/shard_map/ppermute | solution.py:287
  83.4 2.1 %collective-permute-done.refs_1_ = f32[320,128]{1,0:T(8,128)S(1)} collective-permute-done((f32[320,128]{1,0:T(8,128)S(1)}, f32[320,128]{1,0:T(8,128)S(1)}, u32[]{:S(2)}, u32[]{:S(2)}) %collective-permute-start) | collective-permute-done | bytes 163872 | tf_op jit(solution)/shard_map/ppermute | solution.py:287
  85.5 1.6 %shard_map.90 = f32[1280,128]{1,0:T(8,128)} custom-call(f32[320,128]{1,0:T(8,128)S(1)} %get-tuple-element.33.refs_0_, f32[320,128]{1,0:T(8,128)S(1)} %collective-permute-done.refs_1_, f32[320,128]{1,0:T(8,128)S(1)} %collective-permute-done.1.refs_2_, f32[320,128]{1,0:T(8,128)S(1)} %collective-permute-done.2.refs_3_), custom_call_target="tpu_custom_call" | custom-call | tf_op jit(solution)/shard_map/pallas_call | solution.py:241
  87.0 0.0 all-to-all-done.4
  87.0 0.1 reduce_sum.38
  87.1 17.4 %all_to_all.52 = f32[8,8,128]{2,1,0:T(8,128)S(1)} all-to-all(f32[8,8,128]{2,1,0:T(8,128)S(1)} %broadcast_in_dim.28), channel_id=1, replica_groups=mesh['x'=4,'zh'=4,'zl'=4,'y'=4,'core'=2] {'y','core'}, dimensions={0} | all-to-all | bytes 65536 | tf_op jit(solution)/shard_map/all_to_all | solution.py:219
  104.5 0.6 reduce_sum.39
  (4 shorter events, 0.0 us)
Async XLA Ops:
  25.4 24.8 %all-to-all-start.2 = ((f32[4,96,128]{2,1,0:T(8,128)}), f32[4,96,128]{2,1,0:T(8,128)S(1)}, u32[]{:S(2)}, u32[]{:S(2)}) async-start(f32[4,96,128]{2,1,0:T(8,128)} %broadcast_in_dim.12), calls=%async_computation.2 | async-start | bytes 393216 | tf_op jit(solution)/shard_map/all_to_all | solution.py:219
  37.5 21.4 %copy-start = (f32[20,64,64]{2,1,0:T(8,128)S(1)}, f32[20,64,64]{2,1,0:T(8,128)}, u32[]{:S(2)}) copy-start(f32[20,64,64]{2,1,0:T(8,128)} %mix_ref.1) | copy-start | bytes 983044
  37.5 21.4 %copy-start.1 = (s32[512]{0:T(512)S(1)}, s32[512]{0:T(512)}, u32[]{:S(2)}) copy-start(s32[512]{0:T(512)} %own_ref.1) | copy-start | bytes 6148
  65.0 22.1 %all-to-all-start.4 = ((f32[64,8,128]{2,1,0:T(8,128)}), f32[64,8,128]{2,1,0:T(8,128)S(1)}, u32[]{:S(2)}, u32[]{:S(2)}) async-start(f32[64,8,128]{2,1,0:T(8,128)} %bitcast.7), calls=%async_computation.4 | async-start | bytes 524288 | tf_op jit(solution)/shard_map/all_to_all | solution.py:212
  70.8 9.2 %collective-permute-start.2 = (f32[320,128]{1,0:T(8,128)S(1)}, f32[320,128]{1,0:T(8,128)S(1)}, u32[]{:S(2)}, u32[]{:S(2)}) collective-permute-start(f32[320,128]{1,0:T(8,128)S(1)} %get-tuple-element.33.refs_0_), channel_id=1, source_target_pairs={{0,384},{128,0},{256,128},{384,256},{1,385},{129,1},{257,129},{385... | collective-permute-start | bytes 491528 | tf_op jit(solution)/shard_map/ppermute | solution.py:287
  75.2 8.2 %collective-permute-start.1 = (f32[320,128]{1,0:T(8,128)S(1)}, f32[320,128]{1,0:T(8,128)S(1)}, u32[]{:S(2)}, u32[]{:S(2)}) collective-permute-start(f32[320,128]{1,0:T(8,128)S(1)} %get-tuple-element.33.refs_0_), channel_id=1, source_target_pairs={{0,256},{128,384},{256,0},{384,128},{1,257},{129,385},{257,1},{385... | collective-permute-start | bytes 491528 | tf_op jit(solution)/shard_map/ppermute | solution.py:287
  77.5 8.0 %collective-permute-start = (f32[320,128]{1,0:T(8,128)S(1)}, f32[320,128]{1,0:T(8,128)S(1)}, u32[]{:S(2)}, u32[]{:S(2)}) collective-permute-start(f32[320,128]{1,0:T(8,128)S(1)} %get-tuple-element.33.refs_0_), channel_id=1, source_target_pairs={{0,128},{128,256},{256,384},{384,0},{1,129},{129,257},{257,385},{3... | collective-permute-start | bytes 491528 | tf_op jit(solution)/shard_map/ppermute | solution.py:287
where the time goes:
time: 106 us; the launch traced here: 105 us
  blocking collectives  47.6 us (45%)
  starting transfers between devices  27.2 us (26%)
  waiting for transfers between devices  14.5 us (14%)
  Pallas kernels  13.7 us (13%)
    all_to_all x2, blocking collectives, copy_over(): return lax.all_to_all(spread, axes, 0, 0, tiled=True)  26 us
    pallas_call x5, Pallas kernels, call(): pl.pallas_call(kernel, out_shape=tuple((jax.ShapeDtypeStruct(s, t) for s,...  13.7 us
    all_to_all x1, starting transfers between devices, copy_over(): return lax.all_to_all(spread, axes, 0, 0, tiled=True)  12.1 us
    all_to_all x1, blocking collectives, add_over(): swapped = lax.all_to_all(x, axes, 0, 0, tiled=True)  11.1 us
    all_to_all x1, blocking collectives, per_device(): got = lax.all_to_all(packed, 'x', 0, 0, tiled=True)  10.5 us
    ppermute x3, starting transfers between devices, per_device(): lax.ppermute(amp, 'x', [(i, (i + k) % nx) for i in range(nx)])  9.2 us
    all_to_all x1, waiting for transfers between devices, copy_over(): return lax.all_to_all(spread, axes, 0, 0, tiled=True)  9.09 us
    all_to_all x1, starting transfers between devices, add_over(): swapped = lax.all_to_all(x, axes, 0, 0, tiled=True)  5.86 us
  transfers between devices with their start and end apart: 5, of which 3 were waited for; matrix products, arithmetic and copies ran while one was open for 0% of the time, Pallas kernels for 5%

commit v1 on v0

--- a/solution.py
+++ b/solution.py
@@ -110,9 +110,28 @@
     lax.fori_loop(0, dets // GROUP, body, 0, unroll=4)
 
 
+def sum_kernel(count, parts_ref, out_ref):
+    rows = parts_ref.shape[0] // count
+    total = parts_ref[:rows, :]
+    for s in range(1, count):
+        total = total + parts_ref[s * rows:(s + 1) * rows, :]
+    for s in range(out_ref.shape[0] // rows):
+        out_ref[s * rows:(s + 1) * rows, :] = total
+
+
 def weighted_kernel(
-    nx, bands, modes, got_ref, wide_ref, noise_ref, hi_ref, lo_ref, acc_ref, value_s
+    nx, bands, modes, got_ref, own_ref, wide_ref, noise_ref, hi_ref, lo_ref, acc_ref, place_ref, value_s
 ):
+    tiles = place_ref.shape[0]
+    own = own_ref[...]
+    own = jnp.broadcast_to(((own & 1) * HALF + (own >> 1)).astype(F32), (128, tiles))
+    step = min(128, tiles)
+    source = lax.broadcasted_iota(jnp.int32, (step, 2 * HALF), 1).astype(F32)
+    for r in range(0, tiles, step):
+        here = own[:, r:r + step].T[:, 0:1]
+        place_ref[r:r + step, :] = jnp.where(
+            jnp.broadcast_to(here, (step, 2 * HALF)) == source, 1.0, 0.0
+        ).astype(BF16)
     rows = got_ref.shape[0] // nx
     dets = rows - EXTRA
     width = 128 // nx
@@ -147,7 +166,7 @@
 
 
 def correct_kernel(
-    nx, bands, pad, own_ref, proj_ref, mix_ref, wide_ref, noise_ref, hi_ref, lo_ref, start_ref,
+    nx, bands, pad, proj_ref, mix_ref, wide_ref, noise_ref, hi_ref, lo_ref, start_ref, place_ref,
     amp_ref, map_ref, value_s, acc_s
 ):
     modes = mix_ref.shape[1]
@@ -186,9 +205,9 @@
     value_s[...] = -(noise_ref[...] * fitted).astype(BF16).astype(F32)
     acc_s[...] = start_ref[...]
     add_bins(value_s, hi_ref, lo_ref, acc_s)
-    for r in range(map_ref.shape[0]):
-        tile = own_ref[r]
-        map_ref[r:r + 1, :] = acc_s[pl.ds((tile & 1) * HALF + (tile >> 1), 1), :]
+    high, low = split(acc_s[...])
+    placed = jnp.dot(place_ref[...], jnp.concatenate([high, low], axis=1), preferred_element_type=F32)
+    map_ref[...] = placed[:, :TILE_PIX] + placed[:, TILE_PIX:]
 
 
 def gather_kernel(nx, bands, *refs):
@@ -230,7 +249,6 @@
     nz = nh * nl
     nt = lax.axis_size("y") * lax.axis_size("core")
     vmem = pl.BlockSpec(memory_space=pltpu.VMEM)
-    smem = pl.BlockSpec(memory_space=pltpu.SMEM)
     params = pltpu.CompilerParams(vmem_limit_bytes=32 * 1024 * 1024)
 
     bin_cost = pl.CostEstimate(
@@ -263,35 +281,40 @@
     (local,) = call(
         functools.partial(project_kernel, nx, modes, pad), [(nz * pad, 128)], (got,)
     )
-    share, got = lax.optimization_barrier((add_over(local, "zl"), got))
-    wide, noise, hi, lo, start = call(
+    swapped = lax.all_to_all(local, "zl", 0, 0, tiled=True)
+    (copies,) = call(
+        functools.partial(sum_kernel, nl), [(nh * local.shape[0] // nl, 128)], (swapped,)
+    )
+    copies, got = lax.optimization_barrier((copies, got))
+    wide, noise, hi, lo, start, place = call(
         functools.partial(weighted_kernel, nx, bands, modes),
-        [(nx * dets, bands * modes)] + [(dets, times)] * 3 + [(2 * HALF, TILE_PIX)],
-        (got,),
+        [(nx * dets, bands * modes)] + [(dets, times)] * 3 + [(2 * HALF, TILE_PIX), (tiles, 2 * HALF)],
+        (got, ownership[None, :]),
         scratch=[pltpu.VMEM((dets, times), F32)],
         cost=bin_cost,
-        types=[BF16] + [F32] * 4,
-    )
-    share = copy_over(share, "zh").reshape((nh,) + share.shape).sum(0)
-    share, wide, noise, hi, lo, start = lax.optimization_barrier((share, wide, noise, hi, lo, start))
+        types=[BF16] + [F32] * 4 + [BF16],
+    )
+    share = add_over(copies, "zh")
+    share, wide, noise, hi, lo, start, place = lax.optimization_barrier(
+        (share, wide, noise, hi, lo, start, place)
+    )
     projected = copy_over(share, "zl")
     amp, part = call(
         functools.partial(correct_kernel, nx, bands, pad),
         [(bands * modes // nx, 128), (tiles, TILE_PIX)],
-        (ownership, projected, mode_mix, wide, noise, hi, lo, start),
-        specs=[smem] + [vmem] * 7,
+        (projected, mode_mix, wide, noise, hi, lo, start, place),
         scratch=[pltpu.VMEM((dets, times), F32), pltpu.VMEM((2 * HALF, TILE_PIX), F32)],
         cost=bin_cost,
     )
     moved = [
         lax.ppermute(amp, "x", [(i, (i + k) % nx) for i in range(nx)]) for k in range(1, nx)
     ]
+    share = add_over(part, ("x", "zh", "zl"))
+    share, *moved = lax.optimization_barrier((share, *moved))
+    sky_map = copy_over(share, ("y", "core")).reshape((nt,) + share.shape).sum(0)
     (amplitudes,) = call(
         functools.partial(gather_kernel, nx, bands), [(bands * modes, times)], (amp, *moved)
     )
-    share = add_over(part, ("x", "zh", "zl"))
-    share, amplitudes = lax.optimization_barrier((share, amplitudes))
-    sky_map = copy_over(share, ("y", "core")).reshape((nt,) + share.shape).sum(0)
     return amplitudes, sky_map
 
 

time: 106 us -> 105 us (level)
  blocking collectives: 47.6 us -> 30.2 us
  starting transfers between devices: 27.2 us -> 39.8 us
  waiting for transfers between devices: 14.5 us -> 18.4 us
    all_to_all x2 -> x1, blocking collectives: 26 us -> 8.64 us  [copy_over(): return lax.all_to_all(spread, axes, 0, 0, tiled=True)]
    all_to_all x1 -> x2, waiting for transfers between devices: 0.01 us -> 15.2 us  [add_over(): swapped = lax.all_to_all(x, axes, 0, 0, tiled=True)]
    all_to_all x1 -> x2, starting transfers between devices: 5.86 us -> 18 us  [add_over(): swapped = lax.all_to_all(x, axes, 0, 0, tiled=True)]
    all_to_all x1, waiting for transfers between devices: 9.09 us -> 3.13 us  [copy_over(): return lax.all_to_all(spread, axes, 0, 0, tiled=True)]
    ppermute x3, waiting for transfers between devices: 5.41 us -> 0.01 us  [per_device(): lax.ppermute(amp, 'x', [(i, (i + k) % nx) for i in range(nx)])]
    pallas_call x5 -> x6, Pallas kernels: 13.7 us -> 13.5 us  [call(): pl.pallas_call(kernel, out_shape=tuple((jax.ShapeDtypeStruct(s, t) for s,...]
  transfers between devices with their start and end apart: 5 -> 6, of which waited for: 3 -> 3; matrix products, arithmetic and copies ran while one was open for 0% -> 0% of each run, Pallas kernels for 5% -> 5%
where the time goes in v1:
time: 105 us; the launch traced here: 104 us
  starting transfers between devices  39.8 us (38%)
  blocking collectives  30.2 us (29%)
  waiting for transfers between devices  18.4 us (18%)
  Pallas kernels  13.5 us (13%)
    all_to_all x2, starting transfers between devices, add_over(): swapped = lax.all_to_all(x, axes, 0, 0, tiled=True)  18 us
    all_to_all x2, waiting for transfers between devices, add_over(): swapped = lax.all_to_all(x, axes, 0, 0, tiled=True)  15.2 us
    pallas_call x6, Pallas kernels, call(): pl.pallas_call(kernel, out_shape=tuple((jax.ShapeDtypeStruct(s, t) for s,...  13.5 us
    all_to_all x1, starting transfers between devices, copy_over(): return lax.all_to_all(spread, axes, 0, 0, tiled=True)  12.6 us
    all_to_all x1, blocking collectives, per_device(): swapped = lax.all_to_all(local, 'zl', 0, 0, tiled=True)  11.1 us
    all_to_all x1, blocking collectives, per_device(): got = lax.all_to_all(packed, 'x', 0, 0, tiled=True)  10.5 us
    ppermute x3, starting transfers between devices, per_device(): lax.ppermute(amp, 'x', [(i, (i + k) % nx) for i in range(nx)])  9.2 us
    all_to_all x1, blocking collectives, copy_over(): return lax.all_to_all(spread, axes, 0, 0, tiled=True)  8.64 us
  transfers between devices with their start and end apart: 6, of which 3 were waited for; matrix products, arithmetic and copies ran while one was open for 0% of the time, Pallas kernels for 5%

profile of v1, /device:TPU:1, one launch (start us, length us, event | category | flops | bytes accessed | tf_op | source)
XLA Modules:
  0.0 103.9 jit_solution(4717119514822577230)
XLA Ops:
  0.6 0.0 copy-start.1
  0.6 1.8 %shard_map.86 = f32[544,128]{1,0:T(8,128)} custom-call(bf16[64,128]{1,0:T(8,128)(2,1)} %bitcast.18, s32[1,128]{1,0:T(1,128)} %bitcast.19, f32[1,128]{1,0:T(1,128)} %bitcast.20, bf16[128,128]{1,0:T(8,128)(2,1)} %refs_3_.1, s32[128,128]{1,0:T(8,128)} %refs_4_.1), custom_call_target="tpu_custom_call" | custom-call | tf_op jit(solution)/shard_map/pallas_call | solution.py:259
  2.5 10.5 %all_to_all.54 = f32[4,136,128]{2,1,0:T(8,128)S(1)} all-to-all(f32[4,136,128]{2,1,0:T(8,128)} %bitcast.17), channel_id=1, replica_groups=mesh['x'=4,'zh'=4,'zl'=4,'y'=4,'core'=2] {'x'}, dimensions={0} | all-to-all | bytes 557056 | tf_op jit(solution)/shard_map/all_to_all | solution.py:280
  13.0 0.7 shard_map.87
  13.6 11.1 %all_to_all.55 = f32[4,96,128]{2,1,0:T(8,128)S(1)} all-to-all(f32[4,96,128]{2,1,0:T(8,128)S(1)} %bitcast.14), channel_id=1, replica_groups=mesh['x'=4,'zh'=4,'zl'=4,'y'=4,'core'=2] {'zl'}, dimensions={0} | all-to-all | bytes 393216 | tf_op jit(solution)/shard_map/all_to_all | solution.py:284
  24.7 0.7 shard_map.88
  25.4 12.1 %all-to-all-start.2 = ((f32[4,96,128]{2,1,0:T(8,128)}), f32[4,96,128]{2,1,0:T(8,128)S(1)}, u32[]{:S(2)}, u32[]{:S(2)}) async-start(f32[4,96,128]{2,1,0:T(8,128)} %bitcast.7), calls=%async_computation.2 | async-start | bytes 393216 | tf_op jit(solution)/shard_map/all_to_all | solution.py:231
  37.5 0.0 copy-done.1
  37.5 0.0 copy-start
  37.5 3.8 %shard_map.89 = (bf16[512,1280]{1,0:T(8,128)(2,1)S(1)}, f32[128,128]{1,0:T(8,128)S(1)}, f32[128,128]{1,0:T(8,128)S(1)}, f32[128,128]{1,0:T(8,128)S(1)}, f32[512,...) custom-call(f32[544,128]{1,0:T(8,128)S(1)} %bitcast.12, s32[1,512]{1,0:T(1,128)S(1)} %bitcast.16), custom_call_target="tpu_custom_call" | custom-call | flops 2147483648 | bytes 2097152 | tf_op jit(solution)/shard_map/pallas_call | solution.py:259
  41.3 8.9 %all-to-all-done.2 = f32[4,96,128]{2,1,0:T(8,128)S(1)} async-done(((f32[4,96,128]{2,1,0:T(8,128)}), f32[4,96,128]{2,1,0:T(8,128)S(1)}, u32[]{:S(2)}, u32[]{:S(2)}) %all-to-all-start.2) | async-done | bytes 196640 | tf_op jit(solution)/shard_map/all_to_all | solution.py:231
  50.3 8.6 %all_to_all.56 = f32[4,96,128]{2,1,0:T(8,128)S(1)} all-to-all(f32[4,96,128]{2,1,0:T(8,128)S(1)} %broadcast_in_dim.24), channel_id=1, replica_groups=mesh['x'=4,'zh'=4,'zl'=4,'y'=4,'core'=2] {'zl'}, dimensions={0} | all-to-all | bytes 393216 | tf_op jit(solution)/shard_map/all_to_all | solution.py:238
  58.9 0.0 copy-done
  58.9 4.9 %shard_map.90 = (f32[320,128]{1,0:T(8,128)S(1)}, f32[512,128]{1,0:T(8,128)}) custom-call(f32[384,128]{1,0:T(8,128)S(1)} %bitcast.15, f32[20,64,64]{2,1,0:T(8,128)S(1)} %copy-done, bf16[512,1280]{1,0:T(8,128)(2,1)S(1)} %get-tuple-element.32.wide_ref, f32[128,128]{1,0:T(8,128)S(1)} %get-tuple-element.33.noise_ref, f32[128,128]{1,0:T(8,128)S(1)} %get-tuple-element.34.hi_ref, ...), custom_call_target="tpu_custom_call" | custom-call | flops 2147483648 | bytes 2097152 | tf_op jit(solution)/shard_map/pallas_call | solution.py:259
  63.9 5.9 %all-to-all-start.4 = ((f32[64,8,128]{2,1,0:T(8,128)}), f32[64,8,128]{2,1,0:T(8,128)S(1)}, u32[]{:S(2)}, u32[]{:S(2)}) async-start(f32[64,8,128]{2,1,0:T(8,128)} %bitcast.10), calls=%async_computation.4 | async-start | bytes 524288 | tf_op jit(solution)/shard_map/all_to_all | solution.py:231
  69.8 4.3 %collective-permute-start.2 = (f32[320,128]{1,0:T(8,128)S(1)}, f32[320,128]{1,0:T(8,128)S(1)}, u32[]{:S(2)}, u32[]{:S(2)}) collective-permute-start(f32[320,128]{1,0:T(8,128)S(1)} %get-tuple-element.38.refs_0_), channel_id=1, source_target_pairs={{0,384},{128,0},{256,128},{384,256},{1,385},{129,1},{257,129},{385... | collective-permute-start | bytes 491528 | tf_op jit(solution)/shard_map/ppermute | solution.py:310
  74.1 2.3 %collective-permute-start.1 = (f32[320,128]{1,0:T(8,128)S(1)}, f32[320,128]{1,0:T(8,128)S(1)}, u32[]{:S(2)}, u32[]{:S(2)}) collective-permute-start(f32[320,128]{1,0:T(8,128)S(1)} %get-tuple-element.38.refs_0_), channel_id=1, source_target_pairs={{0,256},{128,384},{256,0},{384,128},{1,257},{129,385},{257,1},{385... | collective-permute-start | bytes 491528 | tf_op jit(solution)/shard_map/ppermute | solution.py:310
  76.4 2.6 %collective-permute-start = (f32[320,128]{1,0:T(8,128)S(1)}, f32[320,128]{1,0:T(8,128)S(1)}, u32[]{:S(2)}, u32[]{:S(2)}) collective-permute-start(f32[320,128]{1,0:T(8,128)S(1)} %get-tuple-element.38.refs_0_), channel_id=1, source_target_pairs={{0,128},{128,256},{256,384},{384,0},{1,129},{129,257},{257,385},{3... | collective-permute-start | bytes 491528 | tf_op jit(solution)/shard_map/ppermute | solution.py:310
  79.0 6.3 %all-to-all-done.4 = f32[64,8,128]{2,1,0:T(8,128)S(1)} async-done(((f32[64,8,128]{2,1,0:T(8,128)}), f32[64,8,128]{2,1,0:T(8,128)S(1)}, u32[]{:S(2)}, u32[]{:S(2)}) %all-to-all-start.4) | async-done | bytes 262176 | tf_op jit(solution)/shard_map/all_to_all | solution.py:231
  85.3 0.1 reduce_sum.28
  85.3 0.0 collective-permute-done.2.refs_3_
  85.3 0.0 collective-permute-done.1.refs_2_
  85.3 0.0 collective-permute-done.refs_1_
  85.4 0.6 broadcast_in_dim.25
  86.0 12.6 %all-to-all-start.5 = ((f32[8,8,128]{2,1,0:T(8,128)}), f32[8,8,128]{2,1,0:T(8,128)S(1)}, u32[]{:S(2)}, u32[]{:S(2)}) async-start(f32[8,8,128]{2,1,0:T(8,128)} %broadcast_in_dim.25), calls=%async_computation.5 | async-start | bytes 65536 | tf_op jit(solution)/shard_map/all_to_all | solution.py:238
  98.6 1.6 %shard_map.91 = f32[1280,128]{1,0:T(8,128)} custom-call(f32[320,128]{1,0:T(8,128)S(1)} %get-tuple-element.38.refs_0_, f32[320,128]{1,0:T(8,128)S(1)} %collective-permute-done.refs_1_, f32[320,128]{1,0:T(8,128)S(1)} %collective-permute-done.1.refs_2_, f32[320,128]{1,0:T(8,128)S(1)} %collective-permute-done.2.refs_3_), custom_call_target="tpu_custom_call" | custom-call | tf_op jit(solution)/shard_map/pallas_call | solution.py:259
  100.2 3.1 %all-to-all-done.5 = f32[8,8,128]{2,1,0:T(8,128)S(1)} async-done(((f32[8,8,128]{2,1,0:T(8,128)}), f32[8,8,128]{2,1,0:T(8,128)S(1)}, u32[]{:S(2)}, u32[]{:S(2)}) %all-to-all-start.5) | async-done | bytes 32800 | tf_op jit(solution)/shard_map/all_to_all | solution.py:238
  103.3 0.6 reduce_sum.29
  (2 shorter events, 0.0 us)
Async XLA Ops:
  0.6 36.9 %copy-start.1 = (s32[512]{0:T(512)S(1)}, s32[512]{0:T(512)}, u32[]{:S(2)}) copy-start(s32[512]{0:T(512)} %param.13) | copy-start | bytes 6148
  25.4 24.8 %all-to-all-start.2 = ((f32[4,96,128]{2,1,0:T(8,128)}), f32[4,96,128]{2,1,0:T(8,128)S(1)}, u32[]{:S(2)}, u32[]{:S(2)}) async-start(f32[4,96,128]{2,1,0:T(8,128)} %bitcast.7), calls=%async_computation.2 | async-start | bytes 393216 | tf_op jit(solution)/shard_map/all_to_all | solution.py:231
  37.5 21.4 %copy-start = (f32[20,64,64]{2,1,0:T(8,128)S(1)}, f32[20,64,64]{2,1,0:T(8,128)}, u32[]{:S(2)}) copy-start(f32[20,64,64]{2,1,0:T(8,128)} %mix_ref.1) | copy-start | bytes 983044
  63.9 21.4 %all-to-all-start.4 = ((f32[64,8,128]{2,1,0:T(8,128)}), f32[64,8,128]{2,1,0:T(8,128)S(1)}, u32[]{:S(2)}, u32[]{:S(2)}) async-start(f32[64,8,128]{2,1,0:T(8,128)} %bitcast.10), calls=%async_computation.4 | async-start | bytes 524288 | tf_op jit(solution)/shard_map/all_to_all | solution.py:231
  69.8 15.6 %collective-permute-start.2 = (f32[320,128]{1,0:T(8,128)S(1)}, f32[320,128]{1,0:T(8,128)S(1)}, u32[]{:S(2)}, u32[]{:S(2)}) collective-permute-start(f32[320,128]{1,0:T(8,128)S(1)} %get-tuple-element.38.refs_0_), channel_id=1, source_target_pairs={{0,384},{128,0},{256,128},{384,256},{1,385},{129,1},{257,129},{385... | collective-permute-start | bytes 491528 | tf_op jit(solution)/shard_map/ppermute | solution.py:310
  74.1 11.2 %collective-permute-start.1 = (f32[320,128]{1,0:T(8,128)S(1)}, f32[320,128]{1,0:T(8,128)S(1)}, u32[]{:S(2)}, u32[]{:S(2)}) collective-permute-start(f32[320,128]{1,0:T(8,128)S(1)} %get-tuple-element.38.refs_0_), channel_id=1, source_target_pairs={{0,256},{128,384},{256,0},{384,128},{1,257},{129,385},{257,1},{385... | collective-permute-start | bytes 491528 | tf_op jit(solution)/shard_map/ppermute | solution.py:310
  76.4 9.0 %collective-permute-start = (f32[320,128]{1,0:T(8,128)S(1)}, f32[320,128]{1,0:T(8,128)S(1)}, u32[]{:S(2)}, u32[]{:S(2)}) collective-permute-start(f32[320,128]{1,0:T(8,128)S(1)} %get-tuple-element.38.refs_0_), channel_id=1, source_target_pairs={{0,128},{128,256},{256,384},{384,0},{1,129},{129,257},{257,385},{3... | collective-permute-start | bytes 491528 | tf_op jit(solution)/shard_map/ppermute | solution.py:310
  86.0 17.4 %all-to-all-start.5 = ((f32[8,8,128]{2,1,0:T(8,128)}), f32[8,8,128]{2,1,0:T(8,128)S(1)}, u32[]{:S(2)}, u32[]{:S(2)}) async-start(f32[8,8,128]{2,1,0:T(8,128)} %broadcast_in_dim.25), calls=%async_computation.5 | async-start | bytes 65536 | tf_op jit(solution)/shard_map/all_to_all | solution.py:238
